TPU v7x, 256 devices: a whole 4x4x8 slice. The times are simulated.
256 devices in a mesh: hid: 8 (over x, core), ffn: 32 (over y, z).
Axes of the slice: x: 4, y: 4, z: 8, core: 2. Of those that a mesh axis runs over, the one named last changes fastest.
Arguments:
- states: bfloat16 [512, 16384], P('ffn', 'hid'), may hold values from -6 to 6
- draft_lengths: int32 [64], replicated, may hold values from 1 to 8
- gate_weight: bfloat16 [16384, 28672], P('hid', 'ffn'), may hold values from -0.046875 to 0.046875
- up_weight: bfloat16 [16384, 28672], P('hid', 'ffn'), may hold values from -0.046875 to 0.046875
- down_weight: bfloat16 [28672, 16384], P('ffn', 'hid'), may hold values from -0.03125 to 0.03125
Outputs:
- mixed: float32 [512, 16384], P('ffn', 'hid')
All inputs are finite; a program needn't handle non-finite values.
Results may differ from a plain program's by a relative error of at most 0.0029.
Values may be sent and summed in bfloat16 or wider, within the bound.
A program may use at most 64 MiB of HBM per device.

v0:
```python
import jax
import jax.numpy as jnp
from jax import lax
from jax.sharding import PartitionSpec as P

DRAFT = 8


def activate(both, live_rows):
    units = both.shape[1] // 2
    values = jax.nn.silu(both[:, :units]) * both[:, units:]
    return jnp.where(live_rows[:, None], values, jnp.float32(0.0)).astype(jnp.bfloat16)


def local(states, draft_lengths, gate_weight, up_weight, down_weight):
    steps_draft = DRAFT
    live = (jnp.arange(steps_draft, dtype=jnp.int32)[None, :] < draft_lengths[:, None]).reshape(-1)
    piece = lax.all_gather(states, "ffn", axis=0, tiled=True)
    gate_part = jnp.dot(piece, gate_weight, preferred_element_type=jnp.float32)
    up_part = jnp.dot(piece, up_weight, preferred_element_type=jnp.float32)
    partial_value = jnp.concatenate([gate_part, up_part], axis=1)
    summed = lax.psum(partial_value, "hid")
    hidden = activate(summed, live)
    return lax.psum_scatter(
        jnp.dot(hidden, down_weight, preferred_element_type=jnp.float32),
        "ffn",
        scatter_dimension=0,
        tiled=True,
    )


def solution(mesh):
    placed = (P("ffn", "hid"), P(), P("hid", "ffn"), P("hid", "ffn"), P("ffn", "hid"))
    return jax.shard_map(
        local, mesh=mesh, in_specs=placed, out_specs=P("ffn", "hid"), check_vma=False
    )
```

profile of v0, /device:TPU:1, one launch (start us, length us, event | category | flops | bytes accessed | tf_op | source)
XLA Modules:
  0.0 405.2 jit_solution(7697790739139385877)
XLA Ops:
  6.5 0.0 all-gather.2.cloned.1.call-start
  6.5 0.7 all-gather.2.cloned.1.call-update
  7.3 0.0 all-reduce.2.cloned.1.call-start
  7.3 80.5 %all-gather.2.cloned.1.call-done = bf16[512,2048]{1,0:T(8,128)(2,1)} async-done(((bf16[16,2048]{1,0:T(8,128)(2,1)}), bf16[512,2048]{1,0:T(8,128)(2,1)}) %all-gather.2.cloned.1.call-update) | async-done | bytes 2097168 | tf_op jit(solution)/shard_map/all_gather | solution.py:18
  87.8 0.0 copy-start.1
  87.8 0.0 copy-start.2
  87.8 5.1 %fusion.10 = f32[512,896]{1,0:T(8,128)S(1)} fusion(bf16[512,2048]{1,0:T(8,128)(2,1)} %all-gather.2.cloned.1.call-done, bf16[2048,896]{1,0:T(8,128)(2,1)} %param.8), kind=kOutput, calls=%fused_computation.12 | convolution fusion | flops 1879048192 | bytes 7602176 | tf_op jit(solution)/shard_map/dot_general | solution.py:20
  93.0 0.0 copy-done.1
  93.0 0.0 copy-done.2
  93.0 2.3 fusion.9
  95.3 2.1 pad_maximum_fusion
  97.4 0.0 copy-start
  97.4 0.0 all-reduce.2.cloned.1.call-update
  97.4 0.0 reduce-scatter.2.cloned.1.call-start
  97.5 0.6 copy-done
  98.0 0.1 iota_compare_fusion
  98.1 0.1 lt.23
  98.2 74.6 %all-reduce.2.cloned.1.call-done = f32[512,1792]{1,0:T(8,128)} async-done(((f32[512,1792]{1,0:T(8,128)}), f32[512,1792]{1,0:T(8,128)}) %all-reduce.2.cloned.1.call-update) | async-done | bytes 3670032 | tf_op jit(solution)/shard_map/psum | solution.py:22
  172.8 7.5 %fusion.2 = f32[512,2048]{1,0:T(8,128)} fusion(bf16[896,2048]{1,0:T(8,128)(2,1)} %param.9, f32[512,1792]{1,0:T(8,128)} %all-reduce.2.cloned.1.call-done, pred[512]{0:T(512)(128)(4,1)S(1)} %lt.23), kind=kOutput, calls=%fused_computation.4 | convolution fusion | flops 1882259456 | bytes 11534848 | tf_op jit(solution)/shard_map/dot_general | solution.py:25
  180.3 0.0 reduce-scatter.2.cloned.1.call-update
  180.3 218.3 %reduce-scatter.2.cloned.1.call-done = f32[16,2048]{1,0:T(8,128)} async-done(((f32[512,2048]{1,0:T(8,128)}), f32[16,2048]{1,0:T(8,128)}) %reduce-scatter.2.cloned.1.call-update) | async-done | bytes 131088 | tf_op jit(solution)/shard_map/reduce_scatter | solution.py:24
Async XLA Ops:
  6.5 81.3 %all-gather.2.cloned.1.call-start = ((), (), s32[]{:S(2)}) async-start(), calls=%async_computation.1 | async-start | bytes 2162688 | tf_op jit(solution)/shard_map/all_gather | solution.py:18
  7.3 165.6 %all-reduce.2.cloned.1.call-start = ((), (), s32[]{:S(2)}) async-start(), calls=%async_computation.2 | async-start | bytes 7340032 | tf_op jit(solution)/shard_map/psum | solution.py:22
  87.8 5.2 %copy-start.1 = (bf16[2048,896]{1,0:T(8,128)(2,1)S(1)}, bf16[2048,896]{1,0:T(8,128)(2,1)}, u32[]{:S(2)}) copy-start(bf16[2048,896]{1,0:T(8,128)(2,1)} %param.7) | copy-start | bytes 11010052
  87.8 5.2 %copy-start.2 = (bf16[512,2048]{1,0:T(8,128)(2,1)S(1)}, bf16[512,2048]{1,0:T(8,128)(2,1)}, u32[]{:S(2)}) copy-start(bf16[512,2048]{1,0:T(8,128)(2,1)} %all-gather.2.cloned.1.call-done) | copy-start | bytes 6291460
  97.4 0.7 copy-start
  97.4 301.2 %reduce-scatter.2.cloned.1.call-start = ((), (), s32[]{:S(2)}) async-start(), calls=%async_computation.3 | async-start | bytes 4325376 | tf_op jit(solution)/shard_map/reduce_scatter | solution.py:24
Sparse Core Ops, SparseCore 0:
  9.9 77.8 all-gather.1
  97.5 75.2 all-reduce.1
  180.5 218.1 reduce-scatter.1
where the time goes:
time: 410 us; the launch traced here: 405 us
  waiting for transfers between devices  374 us (91%)
  matrix products  15 us (4%)
  between operations  13.1 us (3%)
    reduce_scatter x1, waiting for transfers between devices, local(): lax.psum_scatter(jnp.dot(hidden, down_weight, preferred_element_type=jnp....  218 us
    all_gather x1, waiting for transfers between devices, local(): piece = lax.all_gather(states, 'ffn', axis=0, tiled=True)  80.5 us
    psum x1, waiting for transfers between devices, local(): summed = lax.psum(partial_value, 'hid')  74.6 us
  transfers between devices with their start and end apart: 3, of which 3 were waited for; matrix products, arithmetic and copies ran while one was open for 0% of the time, Pallas kernels for 0%

commit v1 on v0

v1 whole, which is shorter than its diff:
```python
import jax
import jax.numpy as jnp
from jax import lax
from jax.experimental import pallas as pl
from jax.experimental.pallas import tpu as pltpu
from jax.sharding import PartitionSpec as P

DRAFT = 8
NX, NY, NZ = 4, 4, 8
ROWS = 16
FEAT = 2048
UNITS = 896
BOTH = 2 * UNITS
OUT = 2048
TILE = 256
DY = (0, 1, 3, 2)
DZ_NEAR = (1, 7, 2, 6, 3, 5, 4)
DZ_FAR = (4, 3, 5, 2, 6, 1, 7, 0)


def kernel(
    lengths, states, gate_w, up_w, down_w, out,
    w1, wd, s, part, rc, xs, xr, h, own_out, op, yr, zs, zr,
    w_sem, s_sem, az_s, ay_s, af_s, a_r, c_s, c_r, x_s, x_r, hx_s, hx_r, hc_s, hc_r, y_s, y_r, z_s, z_r,
):
    hid, ffn = lax.axis_index("hid"), lax.axis_index("ffn")
    x, c = hid // 2, hid % 2
    y, z = ffn // NZ, ffn % NZ

    def at_z(dz):
        return (hid, y * NZ + (z + dz) % NZ)

    def at_y(dy):
        return (hid, ((y + dy) % NY) * NZ + z)

    def at_x(dx):
        return (((x + dx) % NX) * 2 + c, ffn)

    mate = (x * 2 + (1 - c), ffn)

    pending = []

    def send(src, dst, send_sem, recv_sem, device):
        copy = pltpu.make_async_remote_copy(src, dst, send_sem, recv_sem, device_id=device)
        copy.start()
        pending.append(copy)

    def arrived(dst, recv_sem):
        pltpu.make_async_remote_copy(dst, dst, w_sem.at[0], recv_sem, device_id=mate).wait_recv()

    mine = pltpu.make_async_copy(states, s.at[y, pl.ds(z * ROWS, ROWS)], s_sem)
    mine.start()
    loads = [
        pltpu.make_async_copy(gate_w, w1.at[:, pl.ds(0, UNITS)], w_sem.at[0]),
        pltpu.make_async_copy(up_w, w1.at[:, pl.ds(UNITS, UNITS)], w_sem.at[1]),
        pltpu.make_async_copy(down_w, wd, w_sem.at[2]),
    ]
    for load in loads:
        load.start()

    barrier = pltpu.get_barrier_semaphore()
    partners = [at_z(d) for d in range(1, NZ)] + [at_y(d) for d in range(1, NY)]
    partners += [at_x(d) for d in range(1, NX)] + [mate]
    for device in partners:
        pl.semaphore_signal(barrier, 1, device_id=device)
    pl.semaphore_wait(barrier, len(partners))
    mine.wait()

    def piece(ya, za):
        return s.at[ya, pl.ds(pl.multiple_of(za * ROWS, ROWS), ROWS)]

    def to_planes(n, za):
        for k, dy in enumerate((1, 3)):
            send(piece(y, za), piece(y, za), ay_s.at[n, k], a_r.at[y, za], at_y(dy))

    def far_plane(n, za):
        sy = (y + 3 + 2 * (za % 2)) % NY
        arrived(piece(sy, za), a_r.at[sy, za])
        dest = (hid, ((y + 1 + 2 * (za % 2)) % NY) * NZ + z)
        send(piece(sy, za), piece(sy, za), af_s.at[n], a_r.at[sy, za], dest)

    to_planes(0, z)
    for n, dz in enumerate(DZ_NEAR):
        send(piece(y, z), piece(y, z), az_s.at[n], a_r.at[y, z], at_z(dz))
    before = z
    for n, dz in enumerate(DZ_NEAR):
        za = (z + dz) % NZ
        arrived(piece(y, za), a_r.at[y, za])
        to_planes(n + 1, za)
        far_plane(n, before)
        before = za

    def first(i):
        ya = (y + DY[i]) % NY

        def tile(n, carry):
            columns = pl.ds(pl.multiple_of(n * TILE, TILE), TILE)
            r = jnp.dot(s[ya], w1[:, columns], preferred_element_type=jnp.float32)
            part[i, :, :, :, columns] = r.reshape(NX, 2, ROWS, TILE)
            return carry

        lax.fori_loop(0, BOTH // TILE, tile, 0)
        send(part.at[i, :, 1 - c], rc.at[i], c_s.at[i], c_r.at[i], mate)

    def over_x(i):
        arrived(rc.at[i], c_r.at[i])
        for dx in range(1, NX):
            xa = (x + dx) % NX
            xs[i, dx - 1] = part[i, xa, c] + rc[i, xa]
            send(xs.at[i, dx - 1], xr.at[i, dx - 1], x_s.at[i, dx - 1], x_r.at[i, dx - 1], at_x(dx))

    def activate(i):
        ya = (y + DY[i]) % NY
        for k in range(NX - 1):
            arrived(xr.at[i, k], x_r.at[i, k])
        both = part[i, x, c] + rc[i, x] + xr[i, 0] + xr[i, 1] + xr[i, 2]
        gate, up = both[:, :UNITS], both[:, UNITS:]
        owner = ya * NZ + hid
        row = lax.broadcasted_iota(jnp.int32, (ROWS, UNITS), 0)
        length = jnp.where(row < DRAFT, lengths[2 * owner], lengths[2 * owner + 1])
        value = gate / (1.0 + jnp.exp(-gate)) * up
        h[i, x, c] = jnp.where(row % DRAFT < length, value, 0.0).astype(jnp.bfloat16)
        for dx in range(1, NX):
            send(h.at[i, x, c], h.at[i, x, c], hx_s.at[i, dx - 1], hx_r.at[i, dx - 1], at_x(dx))

    def to_mate(i):
        for dx in range(1, NX):
            xa = (x + NX - dx) % NX
            arrived(h.at[i, xa, c], hx_r.at[i, dx - 1])
        send(h.at[i, :, c], h.at[i, :, c], hc_s.at[i], hc_r.at[i], mate)

    def second(i):
        arrived(h.at[i, :, 1 - c], hc_r.at[i])

        def tile(n, carry):
            columns = pl.ds(pl.multiple_of(n * TILE, TILE), TILE)
            rows = h[i].reshape(NX * 2 * ROWS, UNITS)
            r = jnp.dot(rows, wd[:, columns], preferred_element_type=jnp.float32)
            if i == 0:
                own_out[:, :, columns] = r.reshape(NZ, ROWS, TILE)
            else:
                op[i - 1, :, :, columns] = r.reshape(NZ, ROWS, TILE).astype(jnp.bfloat16)
            return carry

        lax.fori_loop(0, OUT // TILE, tile, 0)
        if i == 3:
            for n, dz in enumerate(DZ_FAR):
                za = (z + dz) % NZ
                send(op.at[2, za], yr.at[2, za], y_s.at[2, n], y_r.at[2, za], at_y(DY[i]))
        elif i > 0:
            send(op.at[i - 1], yr.at[i - 1], y_s.at[i - 1, 0], y_r.at[i - 1, 0], at_y(DY[i]))

    loads[0].wait()
    loads[1].wait()
    first(0)
    far_plane(7, before)
    for za in range(NZ):
        sy = (y + 1 + 2 * (za % 2)) % NY
        arrived(piece(sy, za), a_r.at[sy, za])
    first(1)
    over_x(0)
    first(2)
    over_x(1)
    for za in range(NZ):
        sy = (y + 2) % NY
        arrived(piece(sy, za), a_r.at[sy, za])
    first(3)
    over_x(2)
    activate(0)
    over_x(3)
    activate(1)
    to_mate(0)
    activate(2)
    to_mate(1)
    loads[2].wait()
    second(0)
    activate(3)
    to_mate(2)
    second(1)
    to_mate(3)
    second(2)
    second(3)

    arrived(yr.at[0], y_r.at[0, 0])
    arrived(yr.at[1], y_r.at[1, 0])
    for dz in DZ_FAR:
        za = (z + dz) % NZ
        arrived(yr.at[2, za], y_r.at[2, za])
        total = own_out[za]
        for k in range(3):
            total = total + yr[k, za].astype(jnp.float32)
        if dz:
            zs[dz - 1] = total.astype(jnp.bfloat16)
            send(zs.at[dz - 1], zr.at[dz - 1], z_s.at[dz - 1], z_r.at[dz - 1], at_z(dz))
        else:
            out[...] = total
    for k in range(NZ - 1):
        arrived(zr.at[k], z_r.at[k])
    total = out[...]
    for k in range(NZ - 1):
        total = total + zr[k].astype(jnp.float32)
    out[...] = total
    for copy in pending:
        copy.wait_send()


def local(states, draft_lengths, gate_weight, up_weight, down_weight):
    f32, bf16 = jnp.float32, jnp.bfloat16
    dma = pltpu.SemaphoreType.DMA
    hbm = pl.BlockSpec(memory_space=pl.ANY)
    return pl.pallas_call(
        kernel,
        out_shape=jax.ShapeDtypeStruct((ROWS, OUT), f32),
        in_specs=[pl.BlockSpec(memory_space=pltpu.SMEM), hbm, hbm, hbm, hbm],
        out_specs=pl.BlockSpec(memory_space=pltpu.VMEM),
        scratch_shapes=[
            pltpu.VMEM((FEAT, BOTH), bf16),
            pltpu.VMEM((UNITS, OUT), bf16),
            pltpu.VMEM((NY, NZ * ROWS, FEAT), bf16),
            pltpu.VMEM((4, NX, 2, ROWS, BOTH), f32),
            pltpu.VMEM((4, NX, ROWS, BOTH), f32),
            pltpu.VMEM((4, NX - 1, ROWS, BOTH), f32),
            pltpu.VMEM((4, NX - 1, ROWS, BOTH), f32),
            pltpu.VMEM((4, NX, 2, ROWS, UNITS), bf16),
            pltpu.VMEM((NZ, ROWS, OUT), f32),
            pltpu.VMEM((3, NZ, ROWS, OUT), bf16),
            pltpu.VMEM((3, NZ, ROWS, OUT), bf16),
            pltpu.VMEM((NZ - 1, ROWS, OUT), bf16),
            pltpu.VMEM((NZ - 1, ROWS, OUT), bf16),
            dma((3,)), dma, dma((7,)), dma((8, 2)), dma((8,)), dma((NY, NZ)),
            dma((4,)), dma((4,)), dma((4, 3)), dma((4, 3)), dma((4, 3)), dma((4, 3)),
            dma((4,)), dma((4,)), dma((3, 8)), dma((3, 8)), dma((7,)), dma((7,)),
        ],
        compiler_params=pltpu.CompilerParams(
            collective_id=0, has_side_effects=True, vmem_limit_bytes=56 << 20
        ),
        cost_estimate=pl.CostEstimate(
            flops=6 * 512 * FEAT * UNITS, bytes_accessed=6 * FEAT * UNITS, transcendentals=64 * UNITS
        ),
    )(draft_lengths, states, gate_weight, up_weight, down_weight)


def solution(mesh):
    placed = (P("ffn", "hid"), P(), P("hid", "ffn"), P("hid", "ffn"), P("ffn", "hid"))
    return jax.shard_map(
        local, mesh=mesh, in_specs=placed, out_specs=P("ffn", "hid"), check_vma=False
    )
```

time: 410 us -> 98.8 us (0.24)
  the two profiles are of different devices: /device:TPU:1 before, /device:TPU:2 now
where the time goes in v1:
time: 98.8 us; the launch traced here: 98.7 us
  Pallas kernels  97.1 us (98%)
  local copies, waits for them, and re-layouts  1.57 us (2%)
    pallas_call x1, Pallas kernels, local(): pl.pallas_call(kernel, out_shape=jax.ShapeDtypeStruct((ROWS, OUT), f32),...  97.1 us

profile of v1, /device:TPU:2, one launch (start us, length us, event | category | flops | bytes accessed | tf_op | source)
XLA Modules:
  0.0 98.7 jit_solution(6687844374592431882)
XLA Ops:
  0.0 97.1 %shard_map.55 = f32[16,2048]{1,0:T(8,128)} custom-call(s32[64]{0:T(128)} %lengths.1, bf16[16,2048]{1,0:T(8,128)(2,1)} %states.1, bf16[2048,896]{1,0:T(8,128)(2,1)} %gate_w.1, bf16[2048,896]{1,0:T(8,128)(2,1)} %up_w.1, bf16[896,2048]{1,0:T(8,128)(2,1)} %down_w.1), custom_call_target="tpu_custom_call" | custom-call | flops 5637144576 | bytes 11010048 | tf_op jit(solution)/shard_map/pallas_call | solution.py:211
  97.1 1.6 %copy.7 = f32[16,2048]{1,0:T(8,128)} copy(f32[16,2048]{1,0:T(8,128)} %shard_map.55) | data formatting | bytes 262144

commit v2 on v0

v2 whole, which is shorter than its diff:
```python
import jax
import jax.numpy as jnp
from jax import lax
from jax.experimental import pallas as pl
from jax.experimental.pallas import tpu as pltpu
from jax.sharding import PartitionSpec as P

DRAFT = 8
NX, NY, NZ = 4, 4, 8
ROWS = 16
FEAT = 2048
UNITS = 896
BOTH = 2 * UNITS
OUT = 2048
TILE = 256
DZ = (7, 0, 5, 2, 3, 4, 1, 6)
OWN = DZ.index(0)
DIRECT = (0, 5, 6, 7)
WIDE = 512
PEERS = ((2, 0), (2, 1), (1, 0), (3, 0), (1, 1), (3, 1), (0, 1))
POWER, SCALE = 7, 128.0


def coded(value):
    a = value * SCALE
    b = a * a * a
    return (b * b * a).astype(jnp.bfloat16)


def decoded(code):
    code = code.astype(jnp.float32)
    size = jnp.exp(jnp.log(jnp.abs(code)) * (1.0 / POWER)) * (1.0 / SCALE)
    return jnp.where(code == 0.0, 0.0, jnp.where(code < 0.0, -size, size))


def kernel(
    lengths, states, gate_w, up_w, down_w, out,
    w1, wd, s, part, rc, xs, xr, h, full, op, ym, mg, yr, zs, zr,
    w_sem, s_sem, az_s, ay_s, a_r, c_s, c_r, x_s, x_r, h_s, h_r, y_s, y_r, z_s, z_r,
):
    hid, ffn = lax.axis_index("hid"), lax.axis_index("ffn")
    x, c = hid // 2, hid % 2
    y, z = ffn // NZ, ffn % NZ

    def at_z(dz):
        return (hid, y * NZ + (z + dz) % NZ)

    def at_y(dy):
        return (hid, ((y + dy) % NY) * NZ + z)

    def at_x(dx):
        return (((x + dx) % NX) * 2 + c, ffn)

    mate = (x * 2 + (1 - c), ffn)
    peers = [(((x + dx) % NX) * 2 + (c + dc) % 2, ffn) for dx, dc in PEERS]

    pending = []

    def send(src, dst, send_sem, recv_sem, device):
        copy = pltpu.make_async_remote_copy(src, dst, send_sem, recv_sem, device_id=device)
        copy.start()
        pending.append(copy)

    def arrived(dst, recv_sem):
        pltpu.make_async_remote_copy(dst, dst, w_sem.at[0], recv_sem, device_id=mate).wait_recv()

    mine = pltpu.make_async_copy(states, s.at[OWN, y], s_sem)
    mine.start()
    loads = [
        pltpu.make_async_copy(gate_w, w1.at[:, pl.ds(0, UNITS)], w_sem.at[0]),
        pltpu.make_async_copy(up_w, w1.at[:, pl.ds(UNITS, UNITS)], w_sem.at[1]),
        pltpu.make_async_copy(down_w, wd, w_sem.at[2]),
    ]
    for load in loads:
        load.start()

    barrier = pltpu.get_barrier_semaphore()
    partners = [at_z(d) for d in range(1, NZ)] + [at_y(d) for d in range(1, NY)]
    partners += peers
    for device in partners:
        pl.semaphore_signal(barrier, 1, device_id=device)
    pl.semaphore_wait(barrier, len(partners))
    mine.wait()

    def to_planes(n):
        if n != OWN:
            arrived(s.at[n, y], a_r.at[n, 0])
        for dy in (2, 1, 3):
            send(s.at[n, y], s.at[n, y], ay_s.at[n, dy - 1], a_r.at[n, dy], at_y(dy))

    def first(n):
        for dy in (1, 3, 2):
            arrived(s.at[n, (y + NY - dy) % NY], a_r.at[n, dy])
        rows = s[n].reshape(NY * ROWS, FEAT)
        for at in range(0, BOTH, TILE):
            r = jnp.dot(rows, w1[:, at : at + TILE], preferred_element_type=jnp.float32)
            for k in range(2):
                low, high = max(at, k * UNITS), min(at + TILE, (k + 1) * UNITS)
                if low < high:
                    part[n, k, :, :, low - k * UNITS : high - k * UNITS] = r[:, low - at : high - at].reshape(
                        NY, ROWS, high - low
                    )
        send(part.at[n, :, :, :, window(1 - c)], rc.at[n], c_s.at[n], c_r.at[n], mate)

    def window(core):
        return pl.ds(pl.multiple_of(core * (UNITS - WIDE), 128), WIDE)

    def over_x(n):
        arrived(rc.at[n], c_r.at[n])
        for dx in (2, 1, 3):
            xa = (x + dx) % NX
            xs[n, dx - 1] = coded(part[n, :, xa, :, window(c)] + rc[n, :, xa])
            send(xs.at[n, dx - 1], xr.at[n, dx - 1], x_s.at[n, dx - 1], x_r.at[n, dx - 1], at_x(dx))

    def activate(n):
        for k in range(NX - 1):
            arrived(xr.at[n, k], x_r.at[n, k])
        both = part[n, :, x, :, window(c)] + rc[n, :, x]
        for k in range(NX - 1):
            both = both + decoded(xr[n, k])
        gate, up = both[0], both[1]
        owner = x * NZ + (z + DZ[n]) % NZ
        row = lax.broadcasted_iota(jnp.int32, (ROWS, WIDE), 0)
        length = jnp.where(row < DRAFT, lengths[2 * owner], lengths[2 * owner + 1])
        value = gate / (1.0 + jnp.exp(-gate)) * up
        h[n, c, x] = jnp.where(row % DRAFT < length, value, 0.0).astype(jnp.bfloat16)
        for k, device in enumerate(peers):
            send(h.at[n, c, x], h.at[n, c, x], h_s.at[n, k], h_r.at[n, k], device)

    def second(n):
        for k, (dx, dc) in enumerate(PEERS):
            arrived(h.at[n, (c + dc) % 2, (x + NX - dx) % NX], h_r.at[n, k])
        low = h[n, 0].reshape(NY * ROWS, WIDE)
        high = h[n, 1].reshape(NY * ROWS, WIDE)[:, 2 * WIDE - UNITS :]
        rows = jnp.concatenate([low, high], axis=1)
        for at in range(0, OUT, TILE):
            r = jnp.dot(rows, wd[:, at : at + TILE], preferred_element_type=jnp.float32)
            r = r.reshape(NY, ROWS, TILE)
            full[n, :, :, at : at + TILE] = r
            op[n, :, :, at : at + TILE] = r.astype(jnp.bfloat16)
        ahead, far, behind = (y + 1) % NY, (y + 2) % NY, (y + 3) % NY
        if n in DIRECT:
            for k, (dy, ya) in enumerate(((2, far), (1, ahead), (3, behind))):
                send(op.at[n, ya], yr.at[n, dy - 1], y_s.at[n, k], y_r.at[n, k], at_y(dy))
        else:
            left, right = pl.ds(0, OUT // 2), pl.ds(OUT // 2, OUT // 2)
            send(op.at[n, far, :, left], ym.at[n, 0], y_s.at[n, 0], y_r.at[n, 0], at_y(1))
            send(op.at[n, far, :, right], ym.at[n, 1], y_s.at[n, 1], y_r.at[n, 1], at_y(3))
            send(op.at[n, ahead, :, right], yr.at[n, 0, :, right], y_s.at[n, 2], y_r.at[n, 2], at_y(1))
            send(op.at[n, behind, :, left], yr.at[n, 1, :, left], y_s.at[n, 3], y_r.at[n, 3], at_y(3))

    def merge(n):
        for k in range(2):
            half = pl.ds(k * (OUT // 2), OUT // 2)
            arrived(ym.at[n, k], y_r.at[n, k])
            near = full[n, (y + 1 + 2 * k) % NY, :, half]
            mg[n, k] = (near + ym[n, k].astype(jnp.float32)).astype(jnp.bfloat16)
            send(mg.at[n, k], yr.at[n, k, :, half], y_s.at[n, 4 + k], y_r.at[n, 4 + k], at_y(1 + 2 * k))

    def over_y(n):
        total = full[n, y]
        if n in DIRECT:
            for k, dy in enumerate((2, 1, 3)):
                arrived(yr.at[n, dy - 1], y_r.at[n, k])
            total = total + yr[n, 2].astype(jnp.float32)
        else:
            for k in range(2):
                half, other = pl.ds(k * (OUT // 2), OUT // 2), pl.ds((1 - k) * (OUT // 2), OUT // 2)
                arrived(yr.at[n, k, :, other], y_r.at[n, 2 + k])
                arrived(yr.at[n, k, :, half], y_r.at[n, 4 + k])
        total = total + yr[n, 0].astype(jnp.float32) + yr[n, 1].astype(jnp.float32)
        if n != OWN:
            k = n - (n > OWN)
            zs[k] = total.astype(jnp.bfloat16)
            send(zs.at[k], zr.at[k], z_s.at[k], z_r.at[k], at_z(DZ[n]))
        else:
            out[...] = total

    for n in range(NZ):
        if n != OWN:
            send(s.at[OWN, y], s.at[n, y], az_s.at[n - (n > OWN)], a_r.at[n, 0], at_z(NZ - DZ[n]))
    to_planes(1)
    to_planes(0)
    loads[0].wait()
    loads[1].wait()
    first(1)
    to_planes(3)
    over_x(1)
    to_planes(2)
    first(0)
    to_planes(4)
    over_x(0)
    activate(1)
    first(3)
    to_planes(5)
    to_planes(7)
    first(2)
    over_x(3)
    activate(0)
    over_x(2)
    to_planes(6)
    loads[2].wait()
    second(1)
    first(4)
    activate(3)
    first(5)
    over_x(4)
    second(0)
    over_x(5)
    activate(2)
    first(7)
    second(3)
    activate(4)
    over_x(7)
    first(6)
    activate(5)
    merge(1)
    second(2)
    over_x(6)
    over_y(0)
    merge(3)
    second(4)
    activate(7)
    over_y(1)
    merge(2)
    second(5)
    over_y(3)
    activate(6)
    merge(4)
    over_y(2)
    second(7)
    over_y(5)
    second(6)
    over_y(4)
    over_y(7)
    over_y(6)
    for k in range(NZ - 1):
        arrived(zr.at[k], z_r.at[k])
    total = out[...]
    for k in range(NZ - 1):
        total = total + zr[k].astype(jnp.float32)
    out[...] = total
    for copy in pending:
        copy.wait_send()


def local(states, draft_lengths, gate_weight, up_weight, down_weight):
    f32, bf16 = jnp.float32, jnp.bfloat16
    dma = pltpu.SemaphoreType.DMA
    hbm = pl.BlockSpec(memory_space=pl.ANY)
    return pl.pallas_call(
        kernel,
        out_shape=jax.ShapeDtypeStruct((ROWS, OUT), f32),
        in_specs=[pl.BlockSpec(memory_space=pltpu.SMEM), hbm, hbm, hbm, hbm],
        out_specs=pl.BlockSpec(memory_space=pltpu.VMEM),
        scratch_shapes=[
            pltpu.VMEM((FEAT, BOTH), bf16),
            pltpu.VMEM((UNITS, OUT), bf16),
            pltpu.VMEM((NZ, NY, ROWS, FEAT), bf16),
            pltpu.VMEM((NZ, 2, NY, ROWS, UNITS), f32),
            pltpu.VMEM((NZ, 2, NY, ROWS, WIDE), f32),
            pltpu.VMEM((NZ, NX - 1, 2, ROWS, WIDE), bf16),
            pltpu.VMEM((NZ, NX - 1, 2, ROWS, WIDE), bf16),
            pltpu.VMEM((NZ, 2, NY, ROWS, WIDE), bf16),
            pltpu.VMEM((NZ, NY, ROWS, OUT), f32),
            pltpu.VMEM((NZ, NY, ROWS, OUT), bf16),
            pltpu.VMEM((NZ, 2, ROWS, OUT // 2), bf16),
            pltpu.VMEM((NZ, 2, ROWS, OUT // 2), bf16),
            pltpu.VMEM((NZ, 3, ROWS, OUT), bf16),
            pltpu.VMEM((NZ - 1, ROWS, OUT), bf16),
            pltpu.VMEM((NZ - 1, ROWS, OUT), bf16),
            dma((3,)), dma, dma((7,)), dma((8, 3)), dma((8, 4)),
            dma((8,)), dma((8,)), dma((8, 3)), dma((8, 3)), dma((8, 7)), dma((8, 7)),
            dma((8, 6)), dma((8, 6)), dma((7,)), dma((7,)),
        ],
        compiler_params=pltpu.CompilerParams(
            collective_id=0, has_side_effects=True, vmem_limit_bytes=56 << 20
        ),
        cost_estimate=pl.CostEstimate(
            flops=6 * 512 * FEAT * UNITS, bytes_accessed=6 * FEAT * UNITS, transcendentals=64 * UNITS
        ),
    )(draft_lengths, states, gate_weight, up_weight, down_weight)


def solution(mesh):
    placed = (P("ffn", "hid"), P(), P("hid", "ffn"), P("hid", "ffn"), P("ffn", "hid"))
    return jax.shard_map(
        local, mesh=mesh, in_specs=placed, out_specs=P("ffn", "hid"), check_vma=False
    )
```

time: 410 us -> 68.6 us (0.17); the launches traced: 405 us -> 68.5 us
  waiting for transfers between devices: 374 us -> 0 us
  Pallas kernels: 0 us -> 66.9 us
  matrix products: 15 us -> 0 us
  between operations: 13.1 us -> 0.01 us
    reduce_scatter x1 -> x0, waiting for transfers between devices: 218 us -> none  [local(): lax.psum_scatter(jnp.dot(hidden, down_weight, preferred_element_type=jnp....]
    all_gather x1 -> x0, waiting for transfers between devices: 80.5 us -> none  [local(): piece = lax.all_gather(states, 'ffn', axis=0, tiled=True)]
    psum x1 -> x0, waiting for transfers between devices: 74.6 us -> none  [local(): summed = lax.psum(partial_value, 'hid')]
    pallas_call x0 -> x1, Pallas kernels: none -> 66.9 us  [local(): pl.pallas_call(kernel, out_shape=jax.ShapeDtypeStruct((ROWS, OUT), f32),...]
    dot_general x3 -> x0, matrix products: 15 us -> none  [the longest x1 7.48 us: local(): jnp.dot(hidden, down_weight, preferred_element_type=jnp.float32)]
  transfers between devices with their start and end apart: 3 -> 0, of which waited for: 3 -> 0; matrix products, arithmetic and copies ran while one was open for 0% -> 0% of each run, Pallas kernels for 0% -> 0%
where the time goes in v2:
time: 68.6 us; the launch traced here: 68.5 us
  Pallas kernels  66.9 us (98%)
  local copies, waits for them, and re-layouts  1.57 us (2%)
    pallas_call x1, Pallas kernels, local(): pl.pallas_call(kernel, out_shape=jax.ShapeDtypeStruct((ROWS, OUT), f32),...  66.9 us
    unnamed x1, local copies, waits for them, and re-layouts  1.57 us

profile of v2, /device:TPU:1, one launch (start us, length us, event | category | flops | bytes accessed | tf_op | source)
XLA Modules:
  0.0 68.5 jit_solution(14238042172267920677)
XLA Ops:
  0.0 66.9 %shard_map.55 = f32[16,2048]{1,0:T(8,128)} custom-call(s32[64]{0:T(128)} %lengths.1, bf16[16,2048]{1,0:T(8,128)(2,1)} %states.1, bf16[2048,896]{1,0:T(8,128)(2,1)} %gate_w.1, bf16[2048,896]{1,0:T(8,128)(2,1)} %up_w.1, bf16[896,2048]{1,0:T(8,128)(2,1)} %down_w.1), custom_call_target="tpu_custom_call" | custom-call | flops 5637144576 | bytes 11010048 | tf_op jit(solution)/shard_map/pallas_call | solution.py:251
  67.0 1.6 %copy.7 = f32[16,2048]{1,0:T(8,128)} copy(f32[16,2048]{1,0:T(8,128)} %shard_map.55) | data formatting | bytes 262144

commit v3 on v2

--- a/solution.py
+++ b/solution.py
@@ -13,7 +13,7 @@
 BOTH = 2 * UNITS
 OUT = 2048
 TILE = 256
-DZ = (7, 0, 5, 2, 3, 4, 1, 6)
+DZ = (7, 0, 2, 5, 3, 4, 1, 6)
 OWN = DZ.index(0)
 DIRECT = (0, 5, 6, 7)
 WIDE = 512
@@ -88,34 +88,35 @@
         for dy in (2, 1, 3):
             send(s.at[n, y], s.at[n, y], ay_s.at[n, dy - 1], a_r.at[n, dy], at_y(dy))
 
-    def first(n):
-        for dy in (1, 3, 2):
-            arrived(s.at[n, (y + NY - dy) % NY], a_r.at[n, dy])
-        rows = s[n].reshape(NY * ROWS, FEAT)
+    def first(*slots):
+        for n in slots:
+            for dy in (1, 3, 2):
+                arrived(s.at[n, (y + NY - dy) % NY], a_r.at[n, dy])
+        span = slice(slots[0], slots[-1] + 1)
+        rows = s[span].reshape(len(slots) * NY * ROWS, FEAT)
         for at in range(0, BOTH, TILE):
             r = jnp.dot(rows, w1[:, at : at + TILE], preferred_element_type=jnp.float32)
+            r = r.reshape(len(slots), NY, ROWS, TILE)
             for k in range(2):
-                low, high = max(at, k * UNITS), min(at + TILE, (k + 1) * UNITS)
-                if low < high:
-                    part[n, k, :, :, low - k * UNITS : high - k * UNITS] = r[:, low - at : high - at].reshape(
-                        NY, ROWS, high - low
-                    )
-        send(part.at[n, :, :, :, window(1 - c)], rc.at[n], c_s.at[n], c_r.at[n], mate)
-
-    def window(core):
-        return pl.ds(pl.multiple_of(core * (UNITS - WIDE), 128), WIDE)
+                for core in range(2):
+                    start = k * UNITS + core * (UNITS - WIDE)
+                    low, high = max(at, start), min(at + TILE, start + WIDE)
+                    if low < high:
+                        part[span, core, k, :, :, low - start : high - start] = r[..., low - at : high - at]
+        for n in slots:
+            send(part.at[n, 1 - c], rc.at[n], c_s.at[n], c_r.at[n], mate)
 
     def over_x(n):
         arrived(rc.at[n], c_r.at[n])
         for dx in (2, 1, 3):
             xa = (x + dx) % NX
-            xs[n, dx - 1] = coded(part[n, :, xa, :, window(c)] + rc[n, :, xa])
+            xs[n, dx - 1] = coded(part[n, c, :, xa] + rc[n, :, xa])
             send(xs.at[n, dx - 1], xr.at[n, dx - 1], x_s.at[n, dx - 1], x_r.at[n, dx - 1], at_x(dx))
 
     def activate(n):
         for k in range(NX - 1):
             arrived(xr.at[n, k], x_r.at[n, k])
-        both = part[n, :, x, :, window(c)] + rc[n, :, x]
+        both = part[n, c, :, x] + rc[n, :, x]
         for k in range(NX - 1):
             both = both + decoded(xr[n, k])
         gate, up = both[0], both[1]
@@ -164,6 +165,7 @@
                 arrived(yr.at[n, dy - 1], y_r.at[n, k])
             total = total + yr[n, 2].astype(jnp.float32)
         else:
+            pass
             for k in range(2):
                 half, other = pl.ds(k * (OUT // 2), OUT // 2), pl.ds((1 - k) * (OUT // 2), OUT // 2)
                 arrived(yr.at[n, k, :, other], y_r.at[n, 2 + k])
@@ -181,67 +183,66 @@
             send(s.at[OWN, y], s.at[n, y], az_s.at[n - (n > OWN)], a_r.at[n, 0], at_z(NZ - DZ[n]))
     to_planes(1)
     to_planes(0)
+    to_planes(2)
     loads[0].wait()
     loads[1].wait()
     first(1)
+    over_x(1)
     to_planes(3)
-    over_x(1)
-    to_planes(2)
     first(0)
     to_planes(4)
     over_x(0)
+    first(2)
     activate(1)
-    first(3)
     to_planes(5)
     to_planes(7)
-    first(2)
+    to_planes(6)
+    over_x(2)
+    first(3)
+    activate(0)
+    first(4)
     over_x(3)
-    activate(0)
-    over_x(2)
-    to_planes(6)
     loads[2].wait()
     second(1)
-    first(4)
-    activate(3)
+    activate(2)
+    over_x(4)
     first(5)
-    over_x(4)
     second(0)
     over_x(5)
-    activate(2)
+    activate(3)
     first(7)
-    second(3)
+    second(2)
     activate(4)
+    merge(1)
     over_x(7)
     first(6)
     activate(5)
-    merge(1)
-    second(2)
+    second(3)
     over_x(6)
     over_y(0)
+    merge(2)
+    second(4)
+    over_y(1)
+    activate(7)
     merge(3)
-    second(4)
-    activate(7)
-    over_y(1)
-    merge(2)
     second(5)
-    over_y(3)
+    over_y(2)
     activate(6)
     merge(4)
-    over_y(2)
     second(7)
+    over_y(3)
     over_y(5)
     second(6)
     over_y(4)
     over_y(7)
     over_y(6)
+    for copy in pending:
+        copy.wait_send()
+    total = out[...]
     for k in range(NZ - 1):
         arrived(zr.at[k], z_r.at[k])
-    total = out[...]
-    for k in range(NZ - 1):
         total = total + zr[k].astype(jnp.float32)
     out[...] = total
-    for copy in pending:
-        copy.wait_send()
 
 
 def local(states, draft_lengths, gate_weight, up_weight, down_weight):
@@ -257,7 +258,7 @@
             pltpu.VMEM((FEAT, BOTH), bf16),
             pltpu.VMEM((UNITS, OUT), bf16),
             pltpu.VMEM((NZ, NY, ROWS, FEAT), bf16),
-            pltpu.VMEM((NZ, 2, NY, ROWS, UNITS), f32),
+            pltpu.VMEM((NZ, 2, 2, NY, ROWS, WIDE), f32),
             pltpu.VMEM((NZ, 2, NY, ROWS, WIDE), f32),
             pltpu.VMEM((NZ, NX - 1, 2, ROWS, WIDE), bf16),
             pltpu.VMEM((NZ, NX - 1, 2, ROWS, WIDE), bf16),

time: 68.6 us -> 67.6 us (0.985)
  Pallas kernels: 66.9 us -> 65.9 us
    pallas_call x1, Pallas kernels: 66.9 us -> 65.9 us  [local(): pl.pallas_call(kernel, out_shape=jax.ShapeDtypeStruct((ROWS, OUT), f32),...]
where the time goes in v3:
time: 67.6 us; the launch traced here: 67.5 us
  Pallas kernels  65.9 us (97%)
  local copies, waits for them, and re-layouts  1.57 us (2%)
    pallas_call x1, Pallas kernels, local(): pl.pallas_call(kernel, out_shape=jax.ShapeDtypeStruct((ROWS, OUT), f32),...  65.9 us
    unnamed x1, local copies, waits for them, and re-layouts  1.57 us

profile of v3, /device:TPU:1, one launch (start us, length us, event | category | flops | bytes accessed | tf_op | source)
XLA Modules:
  0.0 67.5 jit_solution(1230890700491643554)
XLA Ops:
  0.0 65.9 %shard_map.55 = f32[16,2048]{1,0:T(8,128)} custom-call(s32[64]{0:T(128)} %lengths.1, bf16[16,2048]{1,0:T(8,128)(2,1)} %states.1, bf16[2048,896]{1,0:T(8,128)(2,1)} %gate_w.1, bf16[2048,896]{1,0:T(8,128)(2,1)} %up_w.1, bf16[896,2048]{1,0:T(8,128)(2,1)} %down_w.1), custom_call_target="tpu_custom_call" | custom-call | flops 5637144576 | bytes 11010048 | tf_op jit(solution)/shard_map/pallas_call | solution.py:252
  65.9 1.6 %copy.7 = f32[16,2048]{1,0:T(8,128)} copy(f32[16,2048]{1,0:T(8,128)} %shard_map.55) | data formatting | bytes 262144

commit v4 on v3

--- a/solution.py
+++ b/solution.py
@@ -34,7 +34,7 @@
 
 
 def kernel(
-    lengths, states, gate_w, up_w, down_w, out,
+    lengths, states, gate_w, up_w, down_w, out, others,
     w1, wd, s, part, rc, xs, xr, h, full, op, ym, mg, yr, zs, zr,
     w_sem, s_sem, az_s, ay_s, a_r, c_s, c_r, x_s, x_r, h_s, h_r, y_s, y_r, z_s, z_r,
 ):
@@ -238,22 +238,22 @@
     over_y(6)
     for copy in pending:
         copy.wait_send()
-    total = out[...]
+    total = jnp.zeros((ROWS, OUT), jnp.float32)
     for k in range(NZ - 1):
         arrived(zr.at[k], z_r.at[k])
         total = total + zr[k].astype(jnp.float32)
-    out[...] = total
+    others[...] = total
 
 
 def local(states, draft_lengths, gate_weight, up_weight, down_weight):
     f32, bf16 = jnp.float32, jnp.bfloat16
     dma = pltpu.SemaphoreType.DMA
     hbm = pl.BlockSpec(memory_space=pl.ANY)
-    return pl.pallas_call(
+    own, others = pl.pallas_call(
         kernel,
-        out_shape=jax.ShapeDtypeStruct((ROWS, OUT), f32),
+        out_shape=[jax.ShapeDtypeStruct((ROWS, OUT), f32)] * 2,
         in_specs=[pl.BlockSpec(memory_space=pltpu.SMEM), hbm, hbm, hbm, hbm],
-        out_specs=pl.BlockSpec(memory_space=pltpu.VMEM),
+        out_specs=[pl.BlockSpec(memory_space=pltpu.VMEM)] * 2,
         scratch_shapes=[
             pltpu.VMEM((FEAT, BOTH), bf16),
             pltpu.VMEM((UNITS, OUT), bf16),
@@ -281,6 +281,7 @@
             flops=6 * 512 * FEAT * UNITS, bytes_accessed=6 * FEAT * UNITS, transcendentals=64 * UNITS
         ),
     )(draft_lengths, states, gate_weight, up_weight, down_weight)
+    return own + others
 
 
 def solution(mesh):

time: 67.6 us -> 67.7 us (level)
  other arithmetic: 0 us -> 1.64 us
  local copies, waits for them, and re-layouts: 1.57 us -> 0 us
    add x0 -> x1, other arithmetic: none -> 1.64 us  [local(): return own + others]
    unnamed x1 -> x0, local copies, waits for them, and re-layouts: 1.57 us -> none
where the time goes in v4:
time: 67.7 us; the launch traced here: 67.6 us
  Pallas kernels  65.9 us (97%)
  other arithmetic  1.64 us (2%)
    pallas_call x1, Pallas kernels, local(): pl.pallas_call(kernel, out_shape=[jax.ShapeDtypeStruct((ROWS, OUT), f32)]...  65.9 us
    add x1, other arithmetic, local(): return own + others  1.64 us

profile of v4, /device:TPU:1, one launch (start us, length us, event | category | flops | bytes accessed | tf_op | source)
XLA Modules:
  0.0 67.6 jit_solution(3691094886230369346)
XLA Ops:
  0.0 65.9 %shard_map.55 = (f32[16,2048]{1,0:T(8,128)}, f32[16,2048]{1,0:T(8,128)}) custom-call(s32[64]{0:T(128)} %lengths.1, bf16[16,2048]{1,0:T(8,128)(2,1)} %states.1, bf16[2048,896]{1,0:T(8,128)(2,1)} %gate_w.1, bf16[2048,896]{1,0:T(8,128)(2,1)} %up_w.1, bf16[896,2048]{1,0:T(8,128)(2,1)} %down_w.1), custom_call_target="tpu_custom_call" | custom-call | flops 5637144576 | bytes 11010048 | tf_op jit(solution)/shard_map/pallas_call | solution.py:252
  65.9 1.6 %add.3 = f32[16,2048]{1,0:T(8,128)} add(f32[16,2048]{1,0:T(8,128)} %get-tuple-element.7, f32[16,2048]{1,0:T(8,128)} %get-tuple-element.8) | non-fusion elementwise | flops 32768 | bytes 393216 | tf_op jit(solution)/shard_map/add | solution.py:284
